TPU v7x, 32 devices: a whole 2x2x4 slice. The times are simulated.
32 devices in a mesh: groups: 2 (over x), slide: 2 (over core), seq: 8 (over z, y).
Axes of the slice: x: 2, y: 2, z: 4, core: 2. Of those that a mesh axis runs over, the one named last changes fastest.
Arguments:
- held_feats: bfloat16 [4, 8, 1024, 1536], P(('groups', 'slide'), 'seq'), parts along dimension 0, may hold values from -6 to 6
- held_pos: int32 [4, 8, 1024], P(('groups', 'slide'), 'seq'), parts along dimension 0, may hold values from 0 to 4096, as said below
- tile_count: int32 [4], P(('groups', 'slide')), parts along dimension 0, may hold values from 1024 to 4096, as said below
- tile_gain: float32 [1536], replicated, may hold values from 0.25 to 1.75
- w_tile: bfloat16 [1536, 768], replicated, may hold values from -0.15625 to 0.15625
- slide_gain: float32 [768], replicated, may hold values from 0.25 to 1.75
- w_qkv: bfloat16 [768, 2304], replicated, may hold values from -1.5 to 1.5
- w_out: bfloat16 [768, 768], replicated, may hold values from -0.21875 to 0.21875
Outputs:
- slide_out: bfloat16 [4, 4096, 768], P(('groups', 'slide'), 'seq'), parts along dimension 0
There are 2 independent parts, one for each index of `groups`. A program takes and returns all parts, laid end to end along the dimension named above; an argument that names none is the same for every part. Nothing has to cross between parts.
Inputs may be any that keep to these rules, and one draw needn't show every extreme that they name: `held_pos`: slot block d (slots d * 128 to (d + 1) * 128 - 1) of every device holds only positions from d * 512 to (d + 1) * 512 - 1, its live slots first in increasing position, the rest 4096. Each position below the slide's tile_count is held by exactly one slot, no other position by any. `tile_count`: one of the two slides of a part has all 4096 tiles.
All inputs are finite; a program needn't handle non-finite values.
Results may differ from a plain program's by a relative error of at most 0.0025.
The roundings to bfloat16 on the way count: a program that leaves them out, or rounds other values in their place, can miss the bound.
Values may be sent and summed in bfloat16 or wider, within the bound.
A program may use at most 128 MiB of HBM per device.

v0:
```python
import functools
import math

import jax
import jax.numpy as jnp
from jax import lax
from jax.experimental import pallas as pl
from jax.experimental.pallas import tpu as pltpu
from jax.sharding import PartitionSpec as P

SLIDE_WIDTH = 768
HEADS = 16
HEAD_DIM = 48
TILE_DEV = 512
STRIDE = 8
ROWS = TILE_DEV // STRIDE
TILES = 8
LANES = 128
NEGATIVE = -1e30
EPSILON = 1e-06
C = math.log2(math.e) / math.sqrt(HEAD_DIM)
F32 = jnp.float32
BF16 = jnp.bfloat16


def dot(a, b):
    return jnp.dot(a, b, preferred_element_type=F32)


def dot_t(a, b):
    return lax.dot_general(a, b, (((1,), (1,)), ((), ())), preferred_element_type=F32)


def normalise(values, gain):
    center = values - jnp.mean(values, axis=-1, keepdims=True)
    spread = jnp.mean(center * center, axis=-1, keepdims=True)
    return (center * lax.rsqrt(spread + EPSILON) * gain).astype(BF16)


def flip(a, b, size):
    total, bit = 0, 1
    while bit < size:
        total = total + bit * (((a // bit) % 2 + (b // bit) % 2) % 2)
        bit *= 2
    return total


def iota(shape, axis):
    return lax.broadcasted_iota(jnp.int32, shape, axis)


def soft_parts(q, k, v, half_mask, weigh):
    raw = dot_t(q, jnp.where(half_mask, k, jnp.zeros_like(k)))
    top = jnp.max(raw, axis=1, keepdims=True)
    weights = jnp.exp2((raw - top) * C)
    if weigh is not None:
        weights = weights * weigh
    return dot(weights.astype(BF16), v), jnp.sum(weights, axis=1, keepdims=True), top


def kernel(
    n, feats, pos, count, tile_gain, w_tile, slide_gain, w_qkv, w_out, out,
    x_v, wt_v, wq_v, wo_v, wq_pad, wo_pad, emb, arrived, spots, tokens, proj, picks, mids,
    ret_out, ret_in, attn, local_pick,
    x_sem, w_sem, es, er, ps, pr, ms, mr, rs, rr,
):
    me = lax.axis_index("seq")
    groups = n // TILES
    group, mine = me // TILES, me % TILES
    first = me * TILE_DEV
    total = count[0]

    def x_copy(d):
        return pltpu.make_async_copy(feats.at[d], x_v.at[d], x_sem.at[d])

    w_copies = [
        pltpu.make_async_copy(w_tile, wt_v, w_sem.at[0]),
        pltpu.make_async_copy(w_qkv, wq_v, w_sem.at[1]),
        pltpu.make_async_copy(w_out, wo_v, w_sem.at[2]),
    ]
    x_copy(flip(me, n - 1, n)).start()
    w_copies[0].start()

    @pl.loop(1, n)
    def _(i):
        x_copy(flip(me, n - 1 - i, n)).start()

    w_copies[1].start()
    w_copies[2].start()

    barrier = pltpu.get_barrier_semaphore()

    @pl.loop(1, n)
    def _(i):
        pl.semaphore_signal(
            barrier, inc=1, device_id={"seq": (me + i) % n}, device_id_type=pl.DeviceIdType.MESH
        )

    pl.semaphore_wait(barrier, n - 1)

    def remote(src, dst, send, recv, device):
        return pltpu.make_async_remote_copy(
            src_ref=src, dst_ref=dst, send_sem=send, recv_sem=recv,
            device_id={"seq": device}, device_id_type=pl.DeviceIdType.MESH,
        )

    def emb_copy(d, slot):
        return remote(emb.at[d], arrived.at[slot], es.at[d], er.at[slot], d)

    def pos_copy(d, slot):
        return remote(pos.at[d], spots.at[slot], ps.at[d], pr.at[slot], d)

    @pl.loop(0, n - 1)
    def _(i):
        d = flip(me, n - 1 - i, n)
        pos_copy(d, me).start()

    w_copies[0].wait()

    def embed(d):
        x_copy(d).wait()
        normed = normalise(x_v[d].astype(F32), tile_gain[...])
        return dot(normed, wt_v[...]).astype(BF16)

    @pl.loop(0, n - 1)
    def _(i):
        d = flip(me, n - 1 - i, n)
        emb[d] = embed(d)
        emb_copy(d, me).start()

    arrived[me] = embed(me)
    spots[me] = pos[me]

    w_copies[1].wait()
    w_copies[2].wait()

    @pl.loop(0, TILES)
    def _(r):
        def wanted(t):
            half = t // 64
            feature = t % 64
            column = (r + TILES * half) * HEAD_DIM + feature
            return jnp.where(feature < HEAD_DIM, column, -1)

        widen = jnp.where(
            iota((SLIDE_WIDTH, LANES), 0) == wanted(iota((SLIDE_WIDTH, LANES), 1)), 1.0, 0.0
        ).astype(BF16)
        for part in range(3):
            wq_pad[r, :, part * LANES : (part + 1) * LANES] = dot(
                wq_v[:, part * SLIDE_WIDTH : (part + 1) * SLIDE_WIDTH], widen
            ).astype(BF16)
        widen_t = jnp.where(
            iota((LANES, SLIDE_WIDTH), 1) == wanted(iota((LANES, SLIDE_WIDTH), 0)), 1.0, 0.0
        ).astype(BF16)
        wo_pad[r] = dot(widen_t, wo_v[...]).astype(BF16)

    cap = spots.shape[2]

    def place(s):
        hot = jnp.where(iota((TILE_DEV, cap), 0) + first == spots[s], 1.0, 0.0).astype(BF16)
        return dot(hot, arrived[s])

    tokens[...] = place(me)

    @pl.loop(0, n - 1)
    def _(i):
        s = flip(me, n - 1 - i, n)
        pos_copy(s, s).wait_recv()
        emb_copy(s, s).wait_recv()
        tokens[...] += place(s)

    normed = normalise(tokens[...], slide_gain[...])

    def half_lane(shape):
        return iota(shape, 1) % 64

    def gather_rows(r):
        return jnp.where(
            iota((ROWS, TILE_DEV), 1) == STRIDE * iota((ROWS, TILE_DEV), 0) + r, 1.0, 0.0
        ).astype(BF16)

    def mid_copy(r, g, slot):
        d = g * TILES + r
        return remote(picks.at[r], mids.at[slot], ms.at[d], mr.at[slot], d)

    lane3 = iota((TILE_DEV, 3 * LANES), 1)
    is_bias = lane3 % 64 == HEAD_DIM
    valid3 = iota((TILE_DEV, 3 * LANES), 0) + first < total
    bias = jnp.where(
        lane3 < LANES, 1.0, jnp.where((lane3 < 2 * LANES) & (~valid3), NEGATIVE, 0.0)
    )
    extra = jnp.where(is_bias, bias, 0.0)

    def project(r):
        made = (dot(normed, wq_pad[r]) + extra).astype(BF16)
        proj[r] = made
        picked = dot(gather_rows(r), made).astype(BF16)
        return picked

    @pl.loop(0, TILES - 1)
    def _(i):
        r = flip(mine, TILES - 1 - i, TILES)
        picks[r] = project(r)
        for g in range(groups):
            mid_copy(r, g, me).start()

    own_pick = project(mine)
    mids[me] = own_pick
    if groups > 1:
        picks[mine] = own_pick
        for step in range(1, groups):
            mid_copy(mine, (group + step) % groups, me).start()

    lane = iota((TILE_DEV, LANES), 1)
    low = lane < 64

    def half_masks(shape):
        side = iota(shape, 1) < 64
        return side, ~side

    def pack(parts):
        (n0, d0, t0), (n1, d1, t1) = parts
        mixed = jnp.where(low, n0, n1)
        return jnp.where(
            lane == 48, d0, jnp.where(lane == 49, t0,
            jnp.where(lane == 112, d1, jnp.where(lane == 113, t1, mixed))))

    def local_tile(r):
        q = proj[r, :, :LANES]
        k = proj[r, :, LANES : 2 * LANES]
        v = proj[r, :, 2 * LANES :]
        parts = [soft_parts(q, k, v, mask, None) for mask in half_masks(k.shape)]
        (n0, d0, _), (n1, d1, _) = parts
        packed = pack(parts)
        row = iota((TILE_DEV, LANES), 0)
        chosen = row % STRIDE == r
        share = jnp.where(low, n0 / d0, n1 / d1)
        keep = (~chosen) & (row + first < total)
        attn[r] = jnp.where(keep, share, 0.0).astype(BF16)
        local_pick[r] = jnp.sum(
            jnp.where(chosen, packed, 0.0).reshape(ROWS, STRIDE, LANES), axis=1
        )

    before = 5

    @pl.loop(0, before)
    def _(r):
        local_tile(r)

    def ret_copy(t, slot):
        return remote(ret_out.at[t], ret_in.at[slot], rs.at[t], rr.at[slot], group * TILES + t)

    @pl.loop(1, n)
    def _(i):
        s = flip(me, n - i, n)
        remote(mids.at[s], mids.at[s], ms.at[s], mr.at[s], s).wait_recv()

    far_q = mids[pl.ds(group * TILES, TILES), :, :LANES].reshape(TILES * ROWS, LANES)
    far_k = mids[:, :, LANES : 2 * LANES].reshape(n * ROWS, LANES)
    far_v = mids[:, :, 2 * LANES :].reshape(n * ROWS, LANES)
    far_parts = []
    shape = (TILES * ROWS, n * ROWS)
    for half, mask in enumerate(half_masks(far_k.shape)):
        both = (iota(shape, 0) % 2 == half) & (iota(shape, 1) % 2 == half)
        far_parts.append(soft_parts(far_q, far_k, far_v, mask, jnp.where(both, 2.0, 1.0)))
    ret_out[...] = pack(far_parts).reshape(TILES, ROWS, LANES)

    @pl.loop(0, TILES - 1)
    def _(i):
        ret_copy(flip(mine, TILES - 1 - i, TILES), mine).start()

    ret_in[mine] = ret_out[mine]

    @pl.loop(before, TILES)
    def _(r):
        local_tile(r)

    @pl.loop(0, TILES - 1)
    def _(i):
        t = flip(mine, TILES - 1 - i, TILES)
        ret_copy(t, t).wait_recv()

    acc = tokens[...]
    small = iota((ROWS, LANES), 1)
    for r in range(TILES):
        here, there = local_pick[r], ret_in[r]

        def joined(at):
            top = jnp.maximum(here[:, at + 1 : at + 2], there[:, at + 1 : at + 2])
            a = jnp.exp2((here[:, at + 1 : at + 2] - top) * C)
            b = jnp.exp2((there[:, at + 1 : at + 2] - top) * C)
            return (a * here + b * there) / (
                a * here[:, at : at + 1] + b * there[:, at : at + 1]
            )

        share = jnp.where(small < 64, joined(48), joined(112))
        share = jnp.where(small % 64 < HEAD_DIM, share, 0.0)
        valid = iota((ROWS, LANES), 0) * STRIDE + r + first < total
        share = jnp.where(valid, share, 0.0).astype(BF16)
        back = jnp.where(
            iota((TILE_DEV, ROWS), 0) == STRIDE * iota((TILE_DEV, ROWS), 1) + r, 1.0, 0.0
        ).astype(BF16)
        whole = (attn[r].astype(F32) + dot(back, share)).astype(BF16)
        acc = acc + dot(whole, wo_pad[r])
    out[...] = jnp.where(iota((TILE_DEV, 1), 0) + first < total, acc, 0.0).astype(BF16)

    @pl.loop(0, n - 1)
    def _(i):
        d = flip(me, n - 1 - i, n)
        pos_copy(d, me).wait_send()
        emb_copy(d, me).wait_send()
        mid_copy(d % TILES, d // TILES, me).wait_send()

    @pl.loop(0, TILES - 1)
    def _(i):
        ret_copy(flip(mine, TILES - 1 - i, TILES), mine).wait_send()


def shards(n, held_feats, held_pos, tile_count, tile_gain, w_tile, slide_gain, w_qkv, w_out):
    slots, width = held_feats.shape[2:]
    cap = slots // n
    vmem = pl.BlockSpec(memory_space=pltpu.VMEM)
    hbm = pl.BlockSpec(memory_space=pl.ANY)
    smem = pl.BlockSpec(memory_space=pltpu.SMEM)
    dma = pltpu.SemaphoreType.DMA
    result = pl.pallas_call(
        functools.partial(kernel, n),
        out_shape=jax.ShapeDtypeStruct((TILE_DEV, SLIDE_WIDTH), BF16),
        in_specs=[hbm, vmem, smem, vmem, hbm, vmem, hbm, hbm],
        out_specs=vmem,
        scratch_shapes=[
            pltpu.VMEM((n, cap, width), BF16),
            pltpu.VMEM(w_tile.shape, BF16),
            pltpu.VMEM(w_qkv.shape, BF16),
            pltpu.VMEM(w_out.shape, BF16),
            pltpu.VMEM((TILES, SLIDE_WIDTH, 3 * LANES), BF16),
            pltpu.VMEM((TILES, LANES, SLIDE_WIDTH), BF16),
            pltpu.VMEM((n, cap, SLIDE_WIDTH), BF16),
            pltpu.VMEM((n, cap, SLIDE_WIDTH), BF16),
            pltpu.VMEM((n, 1, cap), jnp.int32),
            pltpu.VMEM((TILE_DEV, SLIDE_WIDTH), F32),
            pltpu.VMEM((TILES, TILE_DEV, 3 * LANES), BF16),
            pltpu.VMEM((TILES, ROWS, 3 * LANES), BF16),
            pltpu.VMEM((n, ROWS, 3 * LANES), BF16),
            pltpu.VMEM((TILES, ROWS, LANES), F32),
            pltpu.VMEM((TILES, ROWS, LANES), F32),
            pltpu.VMEM((TILES, TILE_DEV, LANES), BF16),
            pltpu.VMEM((TILES, ROWS, LANES), F32),
            dma((n,)), dma((3,)),
            dma((n,)), dma((n,)), dma((n,)), dma((n,)),
            dma((n,)), dma((n,)), dma((TILES,)), dma((TILES,)),
        ],
        compiler_params=pltpu.CompilerParams(
            collective_id=0, has_side_effects=True, vmem_limit_bytes=58 * 1024 * 1024
        ),
        name="slide_layer",
    )(
        held_feats.reshape(n, cap, width),
        held_pos.reshape(n, 1, cap),
        tile_count,
        tile_gain.reshape(1, width),
        w_tile,
        slide_gain.reshape(1, SLIDE_WIDTH),
        w_qkv,
        w_out,
    )
    return result.reshape(1, TILE_DEV, SLIDE_WIDTH)


def solution(mesh):
    n = mesh.shape["seq"]
    return jax.shard_map(
        functools.partial(shards, n),
        mesh=mesh,
        in_specs=(
            P(("groups", "slide"), "seq", None, None),
            P(("groups", "slide"), "seq", None),
            P(("groups", "slide")),
            P(), P(), P(), P(), P(),
        ),
        out_specs=P(("groups", "slide"), "seq", None),
        check_vma=False,
    )
```

profile of v0, /device:TPU:0, one launch (start us, length us, event | category | flops | bytes accessed | tf_op | source)
XLA Modules:
  0.0 74.0 jit_solution(15311685709148885941)
XLA Ops:
  0.7 1.3 %reshape.18.slide_gain = f32[1,768]{1,0:T(1,128)} reshape(f32[768]{0:T(1024)} %param.13) | data formatting | bytes 6144 | tf_op jit(solution)/shard_map/reshape | solution.py:363
  1.9 1.3 %reshape.17.tile_gain = f32[1,1536]{1,0:T(1,128)} reshape(f32[1536]{0:T(1024)} %param.11) | data formatting | bytes 12288 | tf_op jit(solution)/shard_map/reshape | solution.py:361
  3.2 68.7 %slide_layer.1 = bf16[512,768]{1,0:T(8,128)(2,1)} custom-call(bf16[8,128,1536]{2,1,0:T(8,128)(2,1)} %bitcast.4, s32[8,1,128]{2,1,0:T(1,128)} %bitcast.5, s32[1]{0:T(128)S(6)} %copy.10.count, f32[1,1536]{1,0:T(1,128)} %reshape.17.tile_gain, bf16[1536,768]{1,0:T(8,128)(2,1)} %w_tile.1, f32[1,768]{1,0:T(1,128)} %reshape.18.slide_gain, bf16[768,2304]{1,0:T(8,128)(2,1)} %w_qkv.1, ...), custom_call_target="tpu_custom_call" | custom-call | tf_op jit(solution)/shard_map/slide_layer/pallas_call | solution.py:326
  71.9 2.1 %copy.11 = bf16[1,512,768]{2,1,0:T(8,128)(2,1)} copy(bf16[1,512,768]{2,1,0:T(8,128)(2,1)} %bitcast.3) | data formatting | bytes 1572864
where the time goes:
time: 74.3 us; the launch traced here: 74 us
  Pallas kernels  68.7 us (92%)
  local copies, waits for them, and re-layouts  4.64 us (6%)
    pallas_call x1, Pallas kernels, shards(): pl.pallas_call(functools.partial(kernel, n), out_shape=jax.ShapeDtypeStru...  68.7 us
    unnamed x1, local copies, waits for them, and re-layouts  2.06 us

commit v1 on v0

--- a/solution.py
+++ b/solution.py
@@ -60,8 +60,8 @@
 
 def kernel(
     n, feats, pos, count, tile_gain, w_tile, slide_gain, w_qkv, w_out, out,
-    x_v, wt_v, wq_v, wo_v, wq_pad, wo_pad, emb, arrived, spots, tokens, proj, picks, mids,
-    ret_out, ret_in, attn, local_pick,
+    x_v, wt_v, wq_v, wo_v, wq_pad, wo_pad, emb, arrived, spots, tokens, flat, sorted_rows, picks, mids,
+    ret_out, ret_in, local_pick,
     x_sem, w_sem, es, er, ps, pr, ms, mr, rs, rr,
 ):
     me = lax.axis_index("seq")
@@ -119,7 +119,7 @@
 
     def embed(d):
         x_copy(d).wait()
-        normed = normalise(x_v[d].astype(F32), tile_gain[...])
+        normed = normalise(x_v[d].astype(F32), tile_gain[...][None, :])
         return dot(normed, wt_v[...]).astype(BF16)
 
     @pl.loop(0, n - 1)
@@ -162,40 +162,42 @@
 
     tokens[...] = place(me)
 
-    @pl.loop(0, n - 1)
-    def _(i):
-        s = flip(me, n - 1 - i, n)
+    def take(s):
         pos_copy(s, s).wait_recv()
         emb_copy(s, s).wait_recv()
         tokens[...] += place(s)
 
-    normed = normalise(tokens[...], slide_gain[...])
-
-    def half_lane(shape):
-        return iota(shape, 1) % 64
-
-    def gather_rows(r):
-        return jnp.where(
-            iota((ROWS, TILE_DEV), 1) == STRIDE * iota((ROWS, TILE_DEV), 0) + r, 1.0, 0.0
-        ).astype(BF16)
+    @pl.loop(1, n // 2)
+    def _(i):
+        take(flip(me, i, n))
+
+    @pl.loop(0, n // 2)
+    def _(i):
+        take(flip(me, n - 1 - i, n))
+
+    normed = normalise(tokens[...], slide_gain[...][None, :])
+
+    row_of = iota((TILE_DEV, TILE_DEV), 0)
+    regroup = jnp.where(
+        iota((TILE_DEV, TILE_DEV), 1) == STRIDE * (row_of % ROWS) + row_of // ROWS, 1.0, 0.0
+    ).astype(BF16)
+    sorted_rows[...] = dot(regroup, normed).astype(BF16).reshape(TILES, ROWS, SLIDE_WIDTH)
+    flat[...] = normed
 
     def mid_copy(r, g, slot):
         d = g * TILES + r
         return remote(picks.at[r], mids.at[slot], ms.at[d], mr.at[slot], d)
 
-    lane3 = iota((TILE_DEV, 3 * LANES), 1)
-    is_bias = lane3 % 64 == HEAD_DIM
-    valid3 = iota((TILE_DEV, 3 * LANES), 0) + first < total
-    bias = jnp.where(
-        lane3 < LANES, 1.0, jnp.where((lane3 < 2 * LANES) & (~valid3), NEGATIVE, 0.0)
-    )
-    extra = jnp.where(is_bias, bias, 0.0)
+    def bias(rows, step, start):
+        lane3 = iota((rows, 3 * LANES), 1)
+        valid = iota((rows, 3 * LANES), 0) * step + start + first < total
+        value = jnp.where(
+            lane3 < LANES, 1.0, jnp.where((lane3 < 2 * LANES) & (~valid), NEGATIVE, 0.0)
+        )
+        return jnp.where(lane3 % 64 == HEAD_DIM, value, 0.0)
 
     def project(r):
-        made = (dot(normed, wq_pad[r]) + extra).astype(BF16)
-        proj[r] = made
-        picked = dot(gather_rows(r), made).astype(BF16)
-        return picked
+        return (dot(sorted_rows[r], wq_pad[r]) + bias(ROWS, STRIDE, r)).astype(BF16)
 
     @pl.loop(0, TILES - 1)
     def _(i):
@@ -226,9 +228,10 @@
             jnp.where(lane == 112, d1, jnp.where(lane == 113, t1, mixed))))
 
     def local_tile(r):
-        q = proj[r, :, :LANES]
-        k = proj[r, :, LANES : 2 * LANES]
-        v = proj[r, :, 2 * LANES :]
+        made = (dot(flat[...], wq_pad[r]) + bias(TILE_DEV, 1, 0)).astype(BF16)
+        q = made[:, :LANES]
+        k = made[:, LANES : 2 * LANES]
+        v = made[:, 2 * LANES :]
         parts = [soft_parts(q, k, v, mask, None) for mask in half_masks(k.shape)]
         (n0, d0, _), (n1, d1, _) = parts
         packed = pack(parts)
@@ -236,7 +239,8 @@
         chosen = row % STRIDE == r
         share = jnp.where(low, n0 / d0, n1 / d1)
         keep = (~chosen) & (row + first < total)
-        attn[r] = jnp.where(keep, share, 0.0).astype(BF16)
+        near = jnp.where(keep, share, 0.0).astype(BF16)
+        tokens[...] += dot(near, wo_pad[r])
         local_pick[r] = jnp.sum(
             jnp.where(chosen, packed, 0.0).reshape(ROWS, STRIDE, LANES), axis=1
         )
@@ -280,7 +284,7 @@
         t = flip(mine, TILES - 1 - i, TILES)
         ret_copy(t, t).wait_recv()
 
-    acc = tokens[...]
+    joint = []
     small = iota((ROWS, LANES), 1)
     for r in range(TILES):
         here, there = local_pick[r], ret_in[r]
@@ -297,11 +301,9 @@
         share = jnp.where(small % 64 < HEAD_DIM, share, 0.0)
         valid = iota((ROWS, LANES), 0) * STRIDE + r + first < total
         share = jnp.where(valid, share, 0.0).astype(BF16)
-        back = jnp.where(
-            iota((TILE_DEV, ROWS), 0) == STRIDE * iota((TILE_DEV, ROWS), 1) + r, 1.0, 0.0
-        ).astype(BF16)
-        whole = (attn[r].astype(F32) + dot(back, share)).astype(BF16)
-        acc = acc + dot(whole, wo_pad[r])
+        joint.append(dot(share, wo_pad[r])[:, None, :])
+    added = jnp.concatenate(joint, axis=1).reshape(TILE_DEV, SLIDE_WIDTH)
+    acc = tokens[...] + added
     out[...] = jnp.where(iota((TILE_DEV, 1), 0) + first < total, acc, 0.0).astype(BF16)
 
     @pl.loop(0, n - 1)
@@ -339,12 +341,12 @@
             pltpu.VMEM((n, cap, SLIDE_WIDTH), BF16),
             pltpu.VMEM((n, 1, cap), jnp.int32),
             pltpu.VMEM((TILE_DEV, SLIDE_WIDTH), F32),
-            pltpu.VMEM((TILES, TILE_DEV, 3 * LANES), BF16),
+            pltpu.VMEM((TILE_DEV, SLIDE_WIDTH), BF16),
+            pltpu.VMEM((TILES, ROWS, SLIDE_WIDTH), BF16),
             pltpu.VMEM((TILES, ROWS, 3 * LANES), BF16),
             pltpu.VMEM((n, ROWS, 3 * LANES), BF16),
             pltpu.VMEM((TILES, ROWS, LANES), F32),
             pltpu.VMEM((TILES, ROWS, LANES), F32),
-            pltpu.VMEM((TILES, TILE_DEV, LANES), BF16),
             pltpu.VMEM((TILES, ROWS, LANES), F32),
             dma((n,)), dma((3,)),
             dma((n,)), dma((n,)), dma((n,)), dma((n,)),
@@ -358,9 +360,9 @@
         held_feats.reshape(n, cap, width),
         held_pos.reshape(n, 1, cap),
         tile_count,
-        tile_gain.reshape(1, width),
+        tile_gain,
         w_tile,
-        slide_gain.reshape(1, SLIDE_WIDTH),
+        slide_gain,
         w_qkv,
         w_out,
     )

time: 74.3 us -> 70.9 us (0.954)
  local copies, waits for them, and re-layouts: 4.64 us -> 2.06 us
  Pallas kernels: 68.7 us -> 67.9 us
    reshape x2 -> x0, local copies, waits for them, and re-layouts: 2.57 us -> none  [the longest x1 1.29 us: shards(): tile_gain.reshape(1, width)]
where the time goes in v1:
time: 70.9 us; the launch traced here: 70.7 us
  Pallas kernels  67.9 us (96%)
  local copies, waits for them, and re-layouts  2.06 us (3%)
    pallas_call x1, Pallas kernels, shards(): pl.pallas_call(functools.partial(kernel, n), out_shape=jax.ShapeDtypeStru...  67.9 us
    unnamed x1, local copies, waits for them, and re-layouts  2.06 us

profile of v1, /device:TPU:0, one launch (start us, length us, event | category | flops | bytes accessed | tf_op | source)
XLA Modules:
  0.0 70.7 jit_solution(7612203989946992023)
XLA Ops:
  0.7 67.9 %slide_layer.1 = bf16[512,768]{1,0:T(8,128)(2,1)} custom-call(bf16[8,128,1536]{2,1,0:T(8,128)(2,1)} %bitcast.3, s32[8,1,128]{2,1,0:T(1,128)} %bitcast.5, s32[1]{0:T(128)S(6)} %copy.10.count, f32[1536]{0:T(1024)} %tile_gain.1, bf16[1536,768]{1,0:T(8,128)(2,1)} %w_tile.1, f32[768]{0:T(1024)} %slide_gain.1, bf16[768,2304]{1,0:T(8,128)(2,1)} %w_qkv.1, ...), custom_call_target="tpu_custom_call" | custom-call | tf_op jit(solution)/shard_map/slide_layer/pallas_call | solution.py:328
  68.6 2.1 %copy.11 = bf16[1,512,768]{2,1,0:T(8,128)(2,1)} copy(bf16[1,512,768]{2,1,0:T(8,128)(2,1)} %bitcast.4) | data formatting | bytes 1572864

commit v2 on v1

--- a/solution.py
+++ b/solution.py
@@ -61,7 +61,7 @@
 def kernel(
     n, feats, pos, count, tile_gain, w_tile, slide_gain, w_qkv, w_out, out,
     x_v, wt_v, wq_v, wo_v, wq_pad, wo_pad, emb, arrived, spots, tokens, flat, sorted_rows, picks, mids,
-    ret_out, ret_in, local_pick,
+    ret_out, ret_in, attn, local_pick,
     x_sem, w_sem, es, er, ps, pr, ms, mr, rs, rr,
 ):
     me = lax.axis_index("seq")
@@ -220,12 +220,13 @@
         side = iota(shape, 1) < 64
         return side, ~side
 
-    def pack(parts):
-        (n0, d0, t0), (n1, d1, t1) = parts
-        mixed = jnp.where(low, n0, n1)
+    def blend(parts):
+        return [jnp.where(low, a, b) for a, b in zip(*parts)]
+
+    def pack(number, divisor, top):
         return jnp.where(
-            lane == 48, d0, jnp.where(lane == 49, t0,
-            jnp.where(lane == 112, d1, jnp.where(lane == 113, t1, mixed))))
+            lane % 64 == 48, divisor, jnp.where(lane % 64 == 49, top, number)
+        )
 
     def local_tile(r):
         made = (dot(flat[...], wq_pad[r]) + bias(TILE_DEV, 1, 0)).astype(BF16)
@@ -233,14 +234,14 @@
         k = made[:, LANES : 2 * LANES]
         v = made[:, 2 * LANES :]
         parts = [soft_parts(q, k, v, mask, None) for mask in half_masks(k.shape)]
-        (n0, d0, _), (n1, d1, _) = parts
-        packed = pack(parts)
+        number, divisor, top = blend(parts)
+        packed = pack(number, divisor, top)
         row = iota((TILE_DEV, LANES), 0)
         chosen = row % STRIDE == r
-        share = jnp.where(low, n0 / d0, n1 / d1)
+        share = number / divisor
         keep = (~chosen) & (row + first < total)
-        near = jnp.where(keep, share, 0.0).astype(BF16)
-        tokens[...] += dot(near, wo_pad[r])
+        columns = pl.ds(pl.multiple_of(r * LANES, LANES), LANES)
+        attn[:, columns] = jnp.where(keep, share, 0.0).astype(BF16)
         local_pick[r] = jnp.sum(
             jnp.where(chosen, packed, 0.0).reshape(ROWS, STRIDE, LANES), axis=1
         )
@@ -267,7 +268,7 @@
     for half, mask in enumerate(half_masks(far_k.shape)):
         both = (iota(shape, 0) % 2 == half) & (iota(shape, 1) % 2 == half)
         far_parts.append(soft_parts(far_q, far_k, far_v, mask, jnp.where(both, 2.0, 1.0)))
-    ret_out[...] = pack(far_parts).reshape(TILES, ROWS, LANES)
+    ret_out[...] = pack(*blend(far_parts)).reshape(TILES, ROWS, LANES)
 
     @pl.loop(0, TILES - 1)
     def _(i):
@@ -278,6 +279,8 @@
     @pl.loop(before, TILES)
     def _(r):
         local_tile(r)
+
+    tokens[...] += dot(attn[...], wo_pad[...].reshape(TILES * LANES, SLIDE_WIDTH))
 
     @pl.loop(0, TILES - 1)
     def _(i):
@@ -347,6 +350,7 @@
             pltpu.VMEM((n, ROWS, 3 * LANES), BF16),
             pltpu.VMEM((TILES, ROWS, LANES), F32),
             pltpu.VMEM((TILES, ROWS, LANES), F32),
+            pltpu.VMEM((TILE_DEV, TILES * LANES), BF16),
             pltpu.VMEM((TILES, ROWS, LANES), F32),
             dma((n,)), dma((3,)),
             dma((n,)), dma((n,)), dma((n,)), dma((n,)),

time: 70.9 us -> 70.2 us (level)
  no operation moved by 1% of the time
where the time goes in v2:
time: 70.2 us; the launch traced here: 70 us
  Pallas kernels  67.3 us (96%)
  local copies, waits for them, and re-layouts  2.06 us (3%)
    pallas_call x1, Pallas kernels, shards(): pl.pallas_call(functools.partial(kernel, n), out_shape=jax.ShapeDtypeStru...  67.3 us
    unnamed x1, local copies, waits for them, and re-layouts  2.06 us

profile of v2, /device:TPU:0, one launch (start us, length us, event | category | flops | bytes accessed | tf_op | source)
XLA Modules:
  0.0 70.0 jit_solution(16262205986696078481)
XLA Ops:
  0.7 67.3 %slide_layer.1 = bf16[512,768]{1,0:T(8,128)(2,1)} custom-call(bf16[8,128,1536]{2,1,0:T(8,128)(2,1)} %bitcast.3, s32[8,1,128]{2,1,0:T(1,128)} %bitcast.5, s32[1]{0:T(128)S(6)} %copy.10.count, f32[1536]{0:T(1024)} %tile_gain.1, bf16[1536,768]{1,0:T(8,128)(2,1)} %w_tile.1, f32[768]{0:T(1024)} %slide_gain.1, bf16[768,2304]{1,0:T(8,128)(2,1)} %w_qkv.1, ...), custom_call_target="tpu_custom_call" | custom-call | tf_op jit(solution)/shard_map/slide_layer/pallas_call | solution.py:331
  67.9 2.1 %copy.11 = bf16[1,512,768]{2,1,0:T(8,128)(2,1)} copy(bf16[1,512,768]{2,1,0:T(8,128)(2,1)} %bitcast.4) | data formatting | bytes 1572864
